TPU v7x, 512 devices: a whole 4x8x8 slice. The times are simulated.
512 devices in a mesh: node: 32 (over x, y), chan: 16 (over z, core).
Axes of the slice: x: 4, y: 8, z: 8, core: 2. Of those that a mesh axis runs over, the one named last changes fastest.
Arguments:
- features: bfloat16 [57344, 1024], P('node', 'chan'), may hold values from -0.046875 to 0.046875
- weight: bfloat16 [1024, 1024], P('node', 'chan'), may hold values from -0.375 to 0.375
- pre_clean: bfloat16 [57344, 1024], P('node', 'chan'), may hold values from -6 to 6
- pre_corrupt: bfloat16 [57344, 1024], P('node', 'chan'), may hold values from -6 to 6
- grad_clean: bfloat16 [57344, 1024], P('node', 'chan'), may hold values from -6 to 6
- grad_corrupt: bfloat16 [57344, 1024], P('node', 'chan'), may hold values from -6 to 6
- slopes: float32 [1024], P('chan'), may hold values from 0.05 to 0.5
- adj_vals: bfloat16 [448, 5, 128, 128], P('node'), may hold values from 0 to 0.07861328
- adj_cols: int32 [448, 5], P('node'), may hold values from 0 to 447, as said below
- adj_count: int32 [448], P('node'), may hold values from 1 to 5, as said below
- shuffle_from: int32 [448], replicated, may hold values from 0 to 447, as said below
Outputs:
- grad_weight: float32 [1024, 1024], P('node', 'chan')
- grad_features: bfloat16 [57344, 1024], P('node', 'chan')
Inputs may be any that keep to these rules, and one draw needn't show every extreme that they name: `adj_cols`: entry [b, k] is a block within 2 of b, and entry [b, 0] is b itself. Slots k < adj_count[b] of row block b hold edge tiles; the other slots are padding and are not read. `shuffle_from`: A permutation of the blocks. The 14 blocks of one index of node take their rows from exactly 14 distinct indices of node, 1 block from each; among these are the index just after it and the index 16 away, counted round.
All inputs are finite; a program needn't handle non-finite values.
Results may differ from a plain program's by a relative error of at most 0.023.
Values may be sent and summed in bfloat16 or wider, within the bound.
A program may use at most 64 MiB of HBM per device.

v0:
```python
import jax
import jax.numpy as jnp
from jax import lax
from jax.sharding import PartitionSpec as P


def shifted(value, axis, by):
    size = lax.axis_size(axis)
    pairs = [(i, i + by) for i in range(size) if 0 <= i + by < size]
    return lax.ppermute(value, axis, pairs)


def local_grad(grad_part, pre_part, slopes):
    factor = jnp.where(pre_part > 0, 1.0, slopes[None, :])
    return (grad_part.astype(jnp.float32) * factor).astype(jnp.bfloat16)


def local(
    features,
    weight,
    pre_clean,
    pre_corrupt,
    grad_clean,
    grad_corrupt,
    slopes,
    adj_vals,
    adj_cols,
    adj_count,
    shuffle_from,
):
    row_count, chan_width = features.shape
    blocks = adj_vals.shape[0]
    tile_slots = adj_vals.shape[1]
    tile_rows = adj_vals.shape[2]
    band_reach = (tile_slots - 1) // 2
    my_index = lax.axis_index("node")
    dev_count = lax.axis_size("node")
    d_clean = local_grad(grad_clean, pre_clean, slopes)
    d_corrupt = local_grad(grad_corrupt, pre_corrupt, slopes)
    stacked = jnp.concatenate([d_clean, d_corrupt], axis=1).reshape(
        blocks, tile_rows, 2 * chan_width
    )
    contrib = jnp.einsum("bkpq,bpc->bkqc", adj_vals, stacked, preferred_element_type=jnp.float32)
    span_blocks = blocks + 2 * band_reach
    targets = adj_cols - (my_index * blocks - band_reach)
    live_mask = jnp.arange(tile_slots)[None, :] < adj_count[:, None]
    chooser = (
        (targets.reshape(-1)[None, :] == jnp.arange(span_blocks)[:, None])
        & live_mask.reshape(-1)[None, :]
    ).astype(jnp.float32)
    summed = jnp.dot(
        chooser, contrib.reshape(blocks * tile_slots, -1), precision=lax.Precision.HIGHEST
    )
    summed = summed.reshape(span_blocks, tile_rows, 2 * chan_width)
    from_prev = shifted(summed[band_reach + blocks :].astype(jnp.bfloat16), "node", 1).astype(
        jnp.float32
    )
    from_next = shifted(summed[:band_reach].astype(jnp.bfloat16), "node", -1).astype(jnp.float32)
    remaining = blocks - band_reach
    middle = summed[band_reach : band_reach + blocks]
    middle = (
        middle
        + jnp.pad(from_prev, ((0, remaining), (0, 0), (0, 0)))
        + jnp.pad(from_next, ((remaining, 0), (0, 0), (0, 0)))
    )
    backprop = middle.astype(jnp.bfloat16).reshape(row_count, 2 * chan_width)
    back_clean = backprop[:, :chan_width]
    back_corrupt = backprop[:, chan_width:]
    my_blocks = my_index * blocks + jnp.arange(blocks)
    all_blocks = jnp.arange(shuffle_from.shape[0])
    one_hot = (shuffle_from[None, :] == my_blocks[:, None]).astype(jnp.int32)
    source_block = jnp.sum(one_hot * all_blocks[None, :], axis=1)
    wanted = (source_block[:, None] * tile_rows + jnp.arange(tile_rows)[None, :]).reshape(-1)
    portion = lax.all_gather(back_corrupt, "node", axis=0, tiled=True)
    inside = (wanted >= 0) & (wanted < portion.shape[0])
    fetched = jnp.take(portion, jnp.clip(wanted, 0, portion.shape[0] - 1), axis=0)
    unshuffled = jnp.where(inside[:, None], fetched, jnp.zeros_like(back_corrupt))
    combined = jnp.concatenate([back_clean, unshuffled], axis=1)
    product = lax.dot_general(
        lax.all_gather(features, "chan", axis=1, tiled=True),
        combined,
        (((0,), (0,)), ((), ())),
        preferred_element_type=jnp.float32,
    )
    partial_w = product[:, :chan_width] + product[:, chan_width:]
    share_rows = partial_w.shape[0] // dev_count
    summed_w = lax.psum(partial_w.astype(jnp.bfloat16), "node").astype(jnp.float32)
    grad_weight = lax.dynamic_slice_in_dim(summed_w, my_index * share_rows, share_rows, 0)
    portion = lax.all_gather(weight, "node", axis=0, tiled=True)
    doubled = jnp.concatenate([portion, portion], axis=1)
    partial_x = lax.dot_general(
        combined, doubled, (((1,), (1,)), ((), ())), preferred_element_type=jnp.float32
    )
    grad_features = lax.psum_scatter(
        partial_x.astype(jnp.bfloat16), "chan", scatter_dimension=1, tiled=True
    )
    return (grad_weight, grad_features)


def solution(mesh):
    placed = (
        P("node", "chan"),
        P("node", "chan"),
        P("node", "chan"),
        P("node", "chan"),
        P("node", "chan"),
        P("node", "chan"),
        P("chan"),
        P("node", None, None, None),
        P("node", None),
        P("node"),
        P(),
    )
    return jax.shard_map(
        local,
        mesh=mesh,
        in_specs=placed,
        out_specs=(P("node", "chan"), P("node", "chan")),
        check_vma=False,
    )
```

profile of v0, /device:TPU:2, one launch (start us, length us, event | category | flops | bytes accessed | tf_op | source)
XLA Modules:
  0.0 460.4 jit_solution(3532302501971480463)
XLA Ops:
  7.2 0.0 copy-start
  7.2 0.0 all-gather.3.cloned.1.call-start
  7.2 1.4 copy.28
  8.6 1.2 copy.29
  9.8 1.9 copy.30
  11.7 1.9 copy.31
  13.6 1.5 multiply_convert_fusion.1
  15.2 0.3 pad_maximum_fusion
  15.4 0.0 copy-done
  15.4 2.9 convolution_bitcast_fusion
  18.3 5.7 %copy.33 = f32[14,5,128,128]{3,2,1,0:T(8,128)} copy(f32[14,5,128,128]{2,3,1,0:T(8,128)} %convolution_bitcast_fusion) | data formatting | bytes 9175040 | tf_op jit(solution)/shard_map/bkpq,bpc->bkqc/dot_general | solution.py:43
  24.1 2.9 pad.25
  27.0 0.0 copy-start.2
  27.0 0.0 copy-start.4
  27.0 4.9 %copy.38 = f32[9,8,128,128]{3,1,2,0:T(8,128)} copy(f32[9,8,128,128]{3,2,1,0:T(8,128)S(1)} %bitcast.49) | data formatting | bytes 9437184
  31.9 0.0 copy-done.2
  31.9 0.1 copy.27
  32.0 0.1 eq.28
  32.1 0.0 copy-done.4
  32.1 0.1 iota_compare_fusion.1
  32.2 0.1 lt.58
  32.3 4.1 fusion.24
  36.4 0.1 slice_bitcast_fusion.1
  36.5 3.5 collective-permute-start
  40.0 4.5 collective-permute-start.1
  44.4 0.0 copy-start.1
  44.5 0.1 slice.38
  44.6 0.0 copy-start.3
  44.6 0.2 copy.39
  44.8 0.0 collective-permute-done
  44.8 1.5 collective-permute-done.1
  46.3 0.1 fusion.1
  46.4 1.0 fusion.23
  47.4 0.0 all-gather.3.cloned.1.call-update
  47.4 0.0 all-gather.5.cloned.1.call-start
  47.4 0.7 all-gather.5.cloned.1.call-update
  48.2 0.0 all-reduce.4.cloned.1.call-start
  48.2 0.0 copy-done.1
  48.2 50.6 %all_gather.11 = bf16[1024,64]{1,0:T(8,128)(2,1)S(1)} all-gather(bf16[32,64]{1,0:T(8,128)(2,1)S(1)} %copy-done.1), channel_id=1, replica_groups=mesh['node'=32,'chan'=16] {'node'}, dimensions={0}, use_global_device_ids=true | all-gather | bytes 135168 | tf_op jit(solution)/shard_map/all_gather | solution.py:89
  98.8 0.0 copy-done.3
  98.8 0.2 select_reduce_fusion
  99.0 0.1 fusion.12
  99.1 0.1 fusion.15
  99.2 0.1 fusion.17
  99.3 86.6 %all-gather.3.cloned.1.call-done = bf16[57344,64]{1,0:T(8,128)(2,1)} async-done(((bf16[1792,64]{1,0:T(8,128)(2,1)}), bf16[57344,64]{1,0:T(8,128)(2,1)}) %all-gather.3.cloned.1.call-update) | async-done | bytes 7340048 | tf_op jit(solution)/shard_map/all_gather | solution.py:74
  185.9 11.3 %gather_fusion = bf16[1792,64]{1,0:T(8,128)(2,1)} fusion(bf16[57344,64]{1,0:T(8,128)(2,1)} %all-gather.3.cloned.1.call-done, s32[2048]{0:T(1024)S(1)} %pad_clamp_fusion), kind=kCustom, calls=%fused_computation | custom fusion | bytes 465920 | tf_op jit(solution)/shard_map/jit(_take)/gather | solution.py:76
  197.1 2.7 select_select_fusion
  199.8 32.0 %all-gather.5.cloned.1.call-done = bf16[1792,1024]{0,1:T(8,128)(2,1)} async-done(((bf16[1792,64]{0,1:T(8,128)(2,1)}), bf16[1792,1024]{0,1:T(8,128)(2,1)}) %all-gather.5.cloned.1.call-update) | async-done | bytes 3670032 | tf_op jit(solution)/shard_map/all_gather | solution.py:80
  231.8 3.7 convolution_bitcast_fusion.1
  235.5 0.7 fusion.2
  236.1 0.0 all-reduce.4.cloned.1.call-update
  236.2 0.0 reduce-scatter.2.cloned.1.call-start
  236.2 3.0 convolution_convert_fusion
  239.2 0.0 reduce-scatter.2.cloned.1.call-update
  239.3 147.1 %all-reduce.4.cloned.1.call-done = bf16[1024,64]{0,1:T(8,128)(2,1)} async-done(((bf16[1024,64]{0,1:T(8,128)(2,1)}), bf16[1024,64]{0,1:T(8,128)(2,1)}) %all-reduce.4.cloned.1.call-update) | async-done | bytes 131088 | tf_op jit(solution)/shard_map/psum | solution.py:87
  386.4 0.8 dynamic-slice_convert_fusion
  387.2 0.7 copy.34
  387.9 66.0 %reduce-scatter.2.cloned.1.call-done = bf16[1792,64]{0,1:T(8,128)(2,1)} async-done(((bf16[1792,1024]{0,1:T(8,128)(2,1)}), bf16[1792,64]{0,1:T(8,128)(2,1)}) %reduce-scatter.2.cloned.1.call-update) | async-done | bytes 229392 | tf_op jit(solution)/shard_map/reduce_scatter | solution.py:94
  (7 shorter events, 0.1 us)
Async XLA Ops:
  7.2 8.3 %copy-start = (bf16[14,5,128,128]{3,2,1,0:T(8,128)(2,1)S(1)}, bf16[14,5,128,128]{3,2,1,0:T(8,128)(2,1)}, u32[]{:S(2)}) copy-start(bf16[14,5,128,128]{3,2,1,0:T(8,128)(2,1)} %param.18) | copy-start | bytes 6881284
  7.2 178.7 %all-gather.3.cloned.1.call-start = ((), (), s32[]{:S(2)}) async-start(), calls=%async_computation.1 | async-start | bytes 15138816 | tf_op jit(solution)/shard_map/all_gather | solution.py:74
  27.0 4.9 %copy-start.2 = (s32[14,5]{0,1:T(8,128)S(1)}, s32[14,5]{0,1:T(8,128)}, u32[]{:S(2)}) copy-start(s32[14,5]{0,1:T(8,128)} %param.19) | copy-start | bytes 844
  27.0 5.1 %copy-start.4 = (s32[14]{0:T(128)S(1)}, s32[14]{0:T(128)}, u32[]{:S(2)}) copy-start(s32[14]{0:T(128)} %param.20) | copy-start | bytes 172
  36.5 8.3 %collective-permute-start = (bf16[2,128,128]{2,1,0:T(8,128)(2,1)S(1)}, bf16[2,128,128]{2,1,0:T(8,128)(2,1)S(1)}, u32[]{:S(2)}, u32[]{:S(2)}) collective-permute-start(bf16[2,128,128]{2,1,0:T(8,128)(2,1)S(1)} %bitcast.56), channel_id=1, source_target_pairs={{0,16},{16,32},{32,48},{48,64},{64,80},{80,96},{96,112},{112,128},... | collective-permute-start | bytes 196616 | tf_op jit(solution)/shard_map/ppermute | solution.py:10
  40.0 6.4 %collective-permute-start.1 = (bf16[2,128,128]{2,1,0:T(8,128)(2,1)S(1)}, bf16[2,128,128]{2,1,0:T(8,128)(2,1)S(1)}, u32[]{:S(2)}, u32[]{:S(2)}) collective-permute-start(bf16[2,128,128]{2,1,0:T(8,128)(2,1)S(1)} %bitcast.57), channel_id=1, source_target_pairs={{16,0},{32,16},{48,32},{64,48},{80,64},{96,80},{112,96},{128,112},... | collective-permute-start | bytes 196616 | tf_op jit(solution)/shard_map/ppermute | solution.py:10
  44.4 3.8 copy-start.1
  44.6 54.2 %copy-start.3 = (s32[448]{0:T(512)S(1)}, s32[448]{0:T(512)}, u32[]{:S(2)}) copy-start(s32[448]{0:T(512)} %param.21) | copy-start | bytes 5380
  47.4 184.4 %all-gather.5.cloned.1.call-start = ((), (), s32[]{:S(2)}) async-start(), calls=%async_computation.2 | async-start | bytes 3899392 | tf_op jit(solution)/shard_map/all_gather | solution.py:80
  48.2 338.2 %all-reduce.4.cloned.1.call-start = ((), (), s32[]{:S(2)}) async-start(), calls=%async_computation.3 | async-start | bytes 262144 | tf_op jit(solution)/shard_map/psum | solution.py:87
  236.2 217.7 %reduce-scatter.2.cloned.1.call-start = ((), (), s32[]{:S(2)}) async-start(), calls=%async_computation.4 | async-start | bytes 3899392 | tf_op jit(solution)/shard_map/reduce_scatter | solution.py:94
Sparse Core Ops, SparseCore 0:
  47.5 138.3 all-gather.2
  188.0 43.7 all-gather.4
  236.3 150.0 all-reduce.3
  389.9 63.8 reduce-scatter.1
where the time goes:
time: 461 us; the launch traced here: 460 us
  waiting for transfers between devices  334 us (72%)
  blocking collectives  50.6 us (11%)
  local copies, waits for them, and re-layouts  33.5 us (7%)
  between operations  14 us (3%)
  matrix products  13.7 us (3%)
  starting transfers between devices  8.11 us (2%)
  other arithmetic  6.56 us (1%)
    psum x1, waiting for transfers between devices, local(): lax.psum(partial_w.astype(jnp.bfloat16), 'node').astype(jnp.float32)  147 us
    all_gather x1, waiting for transfers between devices, local(): portion = lax.all_gather(back_corrupt, 'node', axis=0, tiled=True)  86.6 us
    reduce_scatter x1, waiting for transfers between devices, local(): lax.psum_scatter(partial_x.astype(jnp.bfloat16), 'chan', scatter_dimensio...  66 us
    all_gather x1, blocking collectives, local(): portion = lax.all_gather(weight, 'node', axis=0, tiled=True)  50.6 us
    all_gather x1, waiting for transfers between devices, local(): lax.all_gather(features, 'chan', axis=1, tiled=True)  32 us
    unnamed x21, local copies, waits for them, and re-layouts  15.2 us
    gather x1, local copies, waits for them, and re-layouts, local(): jnp.take(portion, jnp.clip(wanted, 0, portion.shape[0] - 1), axis=0)  11.3 us
  transfers between devices with their start and end apart: 6, of which 5 were waited for; matrix products, arithmetic and copies ran while one was open for 4% of the time, Pallas kernels for 0%

commit v1 on v0

--- a/solution.py
+++ b/solution.py
@@ -2,6 +2,18 @@
 import jax.numpy as jnp
 from jax import lax
 from jax.sharding import PartitionSpec as P
+
+
+def page_define(a0):
+    return jnp.concatenate(
+        lax.all_to_all(
+            jnp.stack([a0 for _ in range(lax.axis_size("node"))]),
+            axis_name="node",
+            split_axis=0,
+            concat_axis=0,
+        ),
+        0,
+    )
 
 
 def shifted(value, axis, by):
@@ -71,7 +83,7 @@
     one_hot = (shuffle_from[None, :] == my_blocks[:, None]).astype(jnp.int32)
     source_block = jnp.sum(one_hot * all_blocks[None, :], axis=1)
     wanted = (source_block[:, None] * tile_rows + jnp.arange(tile_rows)[None, :]).reshape(-1)
-    portion = lax.all_gather(back_corrupt, "node", axis=0, tiled=True)
+    portion = page_define(back_corrupt)
     inside = (wanted >= 0) & (wanted < portion.shape[0])
     fetched = jnp.take(portion, jnp.clip(wanted, 0, portion.shape[0] - 1), axis=0)
     unshuffled = jnp.where(inside[:, None], fetched, jnp.zeros_like(back_corrupt))

time: 461 us -> 524 us (1.14)
  blocking collectives: 50.6 us -> 201 us
  waiting for transfers between devices: 334 us -> 221 us
  local copies, waits for them, and re-layouts: 33.5 us -> 49.5 us
  starting transfers between devices: 8.11 us -> 18.5 us
    all_gather x1, blocking collectives: 50.6 us -> 201 us  [local(): portion = lax.all_gather(weight, 'node', axis=0, tiled=True)]
    all_gather x1 -> x0, waiting for transfers between devices: 86.6 us -> none  [local(): portion = lax.all_gather(back_corrupt, 'node', axis=0, tiled=True)]
    all_gather x1, waiting for transfers between devices: 32 us -> 0.02 us  [local(): lax.all_gather(features, 'chan', axis=1, tiled=True)]
    all_to_all x0 -> x1, local copies, waits for them, and re-layouts: none -> 13.8 us  [page_define(): lax.all_to_all(jnp.stack([a0 for _ in range(lax.axis_size('node'))]), axi...]
    all_to_all x0 -> x1, starting transfers between devices: none -> 10.4 us  [page_define(): lax.all_to_all(jnp.stack([a0 for _ in range(lax.axis_size('node'))]), axi...]
    psum x1, waiting for transfers between devices: 147 us -> 153 us  [local(): lax.psum(partial_w.astype(jnp.bfloat16), 'node').astype(jnp.float32)]
    unnamed x21 -> x23, local copies, waits for them, and re-layouts: 15.2 us -> 15.2 us
  transfers between devices with their start and end apart: 6 -> 6, of which waited for: 5 -> 3; matrix products, arithmetic and copies ran while one was open for 4% -> 6% of each run, Pallas kernels for 0% -> 0%
where the time goes in v1:
time: 524 us; the launch traced here: 523 us
  waiting for transfers between devices  221 us (42%)
  blocking collectives  201 us (38%)
  local copies, waits for them, and re-layouts  49.5 us (9%)
  starting transfers between devices  18.5 us (4%)
  between operations  14 us (3%)
  matrix products  13.6 us (3%)
    all_gather x1, blocking collectives, local(): portion = lax.all_gather(weight, 'node', axis=0, tiled=True)  201 us
    psum x1, waiting for transfers between devices, local(): lax.psum(partial_w.astype(jnp.bfloat16), 'node').astype(jnp.float32)  153 us
    reduce_scatter x1, waiting for transfers between devices, local(): lax.psum_scatter(partial_x.astype(jnp.bfloat16), 'chan', scatter_dimensio...  66.2 us
    unnamed x23, local copies, waits for them, and re-layouts  15.2 us
    all_to_all x1, local copies, waits for them, and re-layouts, page_define(): lax.all_to_all(jnp.stack([a0 for _ in range(lax.axis_size('node'))]), axi...  13.8 us
  transfers between devices with their start and end apart: 6, of which 3 were waited for; matrix products, arithmetic and copies ran while one was open for 6% of the time, Pallas kernels for 0%

profile of v1, /device:TPU:2, one launch (start us, length us, event | category | flops | bytes accessed | tf_op | source)
XLA Modules:
  0.0 523.0 jit_solution(9627198795274700671)
XLA Ops:
  7.2 0.0 copy-start
  7.2 1.4 copy.38
  8.5 1.2 copy.39
  9.8 1.9 copy.40
  11.7 1.9 copy.41
  13.6 1.5 multiply_convert_fusion.1
  15.1 0.3 pad_maximum_fusion
  15.4 0.0 copy-done
  15.4 2.9 convolution_bitcast_fusion
  18.3 5.7 %copy.43 = f32[14,5,128,128]{3,2,1,0:T(8,128)} copy(f32[14,5,128,128]{2,3,1,0:T(8,128)} %convolution_bitcast_fusion) | data formatting | bytes 9175040 | tf_op jit(solution)/shard_map/bkpq,bpc->bkqc/dot_general | solution.py:55
  24.0 2.9 pad.25
  27.0 0.0 copy-start.3
  27.0 0.0 copy-start.5
  27.0 4.9 copy.50
  31.8 0.0 copy-done.3
  31.8 0.1 copy.37
  31.9 0.1 eq.28
  32.0 0.0 copy-done.5
  32.0 0.1 iota_compare_fusion.1
  32.1 0.1 lt.58
  32.2 4.0 fusion.24
  36.3 0.1 slice_bitcast_fusion.1
  36.4 3.5 collective-permute-start
  39.9 4.5 collective-permute-start.1
  44.3 0.1 slice.38
  44.4 0.2 copy.51
  44.7 0.0 collective-permute-done
  44.7 1.6 collective-permute-done.1
  46.2 0.1 fusion.1
  46.3 0.2 fusion.23
  46.5 0.2 copy.44
  46.7 3.8 stack.2
  50.5 0.0 copy-start.2
  50.5 0.0 copy-start.4
  50.5 10.4 %all-to-all-start = ((bf16[32,1792,64]{1,2,0:T(8,128)(2,1)}), bf16[32,1792,64]{1,2,0:T(8,128)(2,1)}, u32[]{:S(2)}, u32[]{:S(2)}) async-start(bf16[32,1792,64]{1,2,0:T(8,128)(2,1)} %stack.2), calls=%async_computation | async-start | bytes 14680064 | tf_op jit(solution)/shard_map/all_to_all | solution.py:9
  60.9 0.0 all-gather.2.cloned.1.call-start
  61.0 0.7 all-gather.2.cloned.1.call-update
  61.7 0.0 all-reduce.4.cloned.1.call-start
  61.7 0.0 copy-done.2
  61.7 200.8 %all_gather.7 = bf16[1024,64]{1,0:T(8,128)(2,1)S(1)} all-gather(bf16[32,64]{1,0:T(8,128)(2,1)S(1)} %copy-done.2), channel_id=1, replica_groups=mesh['node'=32,'chan'=16] {'node'}, dimensions={0}, use_global_device_ids=true | all-gather | bytes 135168 | tf_op jit(solution)/shard_map/all_gather | solution.py:101
  262.5 0.0 copy-done.4
  262.5 0.2 select_reduce_fusion
  262.7 0.1 fusion.12
  262.9 0.1 fusion.15
  262.9 0.1 fusion.17
  263.0 0.0 all-to-all-done
  263.0 13.8 %copy.45 = bf16[32,1792,64]{2,1,0:T(8,128)(2,1)} copy(bf16[32,1792,64]{1,2,0:T(8,128)(2,1)} %all-to-all-done) | data formatting | bytes 14680064 | tf_op jit(solution)/shard_map/all_to_all | solution.py:9
  276.9 10.2 %gather_fusion = bf16[1792,64]{1,0:T(8,128)(2,1)S(1)} fusion(bf16[57344,64]{1,0:T(8,128)(2,1)} %bitcast.50, s32[2048]{0:T(1024)S(1)} %pad_clamp_fusion), kind=kCustom, calls=%fused_computation | custom fusion | bytes 465920 | tf_op jit(solution)/shard_map/jit(_take)/gather | solution.py:88
  287.1 1.3 select_select_fusion
  288.4 0.0 all-gather.2.cloned.1.call-done
  288.4 3.7 convolution_bitcast_fusion.1
  292.1 0.7 fusion.2
  292.8 0.0 all-reduce.4.cloned.1.call-update
  292.8 0.0 copy-start.1
  292.8 0.0 reduce-scatter.2.cloned.1.call-start
  292.9 3.0 convolution_convert_fusion
  295.9 0.0 reduce-scatter.2.cloned.1.call-update
  296.0 152.8 %all-reduce.4.cloned.1.call-done = bf16[1024,64]{0,1:T(8,128)(2,1)} async-done(((bf16[1024,64]{0,1:T(8,128)(2,1)}), bf16[1024,64]{0,1:T(8,128)(2,1)}) %all-reduce.4.cloned.1.call-update) | async-done | bytes 131088 | tf_op jit(solution)/shard_map/psum | solution.py:99
  448.8 0.8 dynamic-slice_convert_fusion
  449.6 0.7 copy.46
  450.3 66.2 %reduce-scatter.2.cloned.1.call-done = bf16[1792,64]{0,1:T(8,128)(2,1)} async-done(((bf16[1792,1024]{0,1:T(8,128)(2,1)}), bf16[1792,64]{0,1:T(8,128)(2,1)}) %reduce-scatter.2.cloned.1.call-update) | async-done | bytes 229392 | tf_op jit(solution)/shard_map/reduce_scatter | solution.py:106
  516.4 0.0 copy-done.1
  (7 shorter events, 0.1 us)
Async XLA Ops:
  7.2 8.2 %copy-start = (bf16[14,5,128,128]{3,2,1,0:T(8,128)(2,1)S(1)}, bf16[14,5,128,128]{3,2,1,0:T(8,128)(2,1)}, u32[]{:S(2)}) copy-start(bf16[14,5,128,128]{3,2,1,0:T(8,128)(2,1)} %param.18) | copy-start | bytes 6881284
  27.0 4.9 copy-start.3
  27.0 5.1 copy-start.5
  36.4 8.3 %collective-permute-start = (bf16[2,128,128]{2,1,0:T(8,128)(2,1)S(1)}, bf16[2,128,128]{2,1,0:T(8,128)(2,1)S(1)}, u32[]{:S(2)}, u32[]{:S(2)}) collective-permute-start(bf16[2,128,128]{2,1,0:T(8,128)(2,1)S(1)} %bitcast.58), channel_id=1, source_target_pairs={{0,16},{16,32},{32,48},{48,64},{64,80},{80,96},{96,112},{112,128},... | collective-permute-start | bytes 196616 | tf_op jit(solution)/shard_map/ppermute | solution.py:22
  39.9 6.4 %collective-permute-start.1 = (bf16[2,128,128]{2,1,0:T(8,128)(2,1)S(1)}, bf16[2,128,128]{2,1,0:T(8,128)(2,1)S(1)}, u32[]{:S(2)}, u32[]{:S(2)}) collective-permute-start(bf16[2,128,128]{2,1,0:T(8,128)(2,1)S(1)} %bitcast.59), channel_id=1, source_target_pairs={{16,0},{32,16},{48,32},{64,48},{80,64},{96,80},{112,96},{128,112},... | collective-permute-start | bytes 196616 | tf_op jit(solution)/shard_map/ppermute | solution.py:22
  50.5 11.2 %copy-start.2 = (bf16[32,64]{1,0:T(8,128)(2,1)S(1)}, bf16[32,64]{1,0:T(8,128)(2,1)}, u32[]{:S(2)}) copy-start(bf16[32,64]{1,0:T(8,128)(2,1)} %param.12) | copy-start | bytes 12292
  50.5 212.0 %copy-start.4 = (s32[448]{0:T(512)S(1)}, s32[448]{0:T(512)}, u32[]{:S(2)}) copy-start(s32[448]{0:T(512)} %param.21) | copy-start | bytes 5380
  50.5 212.5 %all-to-all-start = ((bf16[32,1792,64]{1,2,0:T(8,128)(2,1)}), bf16[32,1792,64]{1,2,0:T(8,128)(2,1)}, u32[]{:S(2)}, u32[]{:S(2)}) async-start(bf16[32,1792,64]{1,2,0:T(8,128)(2,1)} %stack.2), calls=%async_computation | async-start | bytes 14680064 | tf_op jit(solution)/shard_map/all_to_all | solution.py:9
  60.9 227.5 %all-gather.2.cloned.1.call-start = ((), (), s32[]{:S(2)}) async-start(), calls=%async_computation.2 | async-start | bytes 3899392 | tf_op jit(solution)/shard_map/all_gather | solution.py:92
  61.7 387.1 %all-reduce.4.cloned.1.call-start = ((), (), s32[]{:S(2)}) async-start(), calls=%async_computation.3 | async-start | bytes 262144 | tf_op jit(solution)/shard_map/psum | solution.py:99
  292.8 223.6 %copy-start.1 = (bf16[14,5,128,128]{3,2,1,0:T(8,128)(2,1)S(1)}, bf16[14,5,128,128]{3,2,1,0:T(8,128)(2,1)}, u32[]{:S(2)}) copy-start(bf16[14,5,128,128]{3,2,1,0:T(8,128)(2,1)} %param.18) | copy-start | bytes 6881284
  292.8 223.6 %reduce-scatter.2.cloned.1.call-start = ((), (), s32[]{:S(2)}) async-start(), calls=%async_computation.4 | async-start | bytes 3899392 | tf_op jit(solution)/shard_map/reduce_scatter | solution.py:106
Sparse Core Ops, SparseCore 0:
  63.9 49.0 all-gather.1
  293.0 155.7 all-reduce.3
  452.5 63.8 reduce-scatter.1
